TPU v7x, 256 devices: a whole 4x4x8 slice. The times are simulated.
256 devices in a mesh: grp: 16 (over y_hi, z), uly: 4 (over x), blk: 4 (over y_lo, core).
Axes of the slice: x: 4, y: 4 (y_hi: 2, y_lo: 2; y = y_hi * 2 + y_lo), z: 8, core: 2. Of those that a mesh axis runs over, the one named last changes fastest.
Arguments:
- q_in: bfloat16 [16, 3072, 2560], P(None, ('grp', 'uly', 'blk')), may hold values from -80 to 80
- k_in: bfloat16 [16, 3072, 2560], P(None, ('grp', 'uly', 'blk')), may hold values from -80 to 80
- v_in: bfloat16 [16, 3072, 2560], P(None, ('grp', 'uly', 'blk')), may hold values from -6 to 6
- q_gain: float32 [2560], replicated, may hold values from 1 to 3
- k_gain: float32 [2560], replicated, may hold values from 1 to 3
- lengths: int32 [16], replicated, may hold values from 1 to 3072, 30720 in all
Outputs:
- attended: bfloat16 [16, 3072, 2560], P(None, ('grp', 'uly', 'blk'))
All inputs are finite; a program needn't handle non-finite values.
Results may differ from a plain program's by a relative error of at most 0.012.
The roundings to bfloat16 on the way count: a program that leaves them out, or rounds other values in their place, can miss the bound.
Values may be sent and summed in bfloat16 or wider, within the bound.
A program may use at most 128 MiB of HBM per device.

v0:
```python
import functools
import math

import jax
import jax.numpy as jnp
from jax import lax
from jax.experimental import pallas as pl
from jax.experimental.pallas import tpu as pltpu
from jax.sharding import PartitionSpec as P

HD = 128
T = 12
R = 16
HALF = 1280
SLOTS = 64
KEYS = 3072
TILE = 384
BLOCK = 768
SUB = 256
REACH = 1536
CUT = 10
LOG2E = math.log2(math.e)
MESH = pl.DeviceIdType.MESH
BF = jnp.bfloat16
F32 = jnp.float32


def slot_pos(shape, slot, zpar):
    w = lax.broadcasted_iota(jnp.int32, shape, 1)
    cc = (w >= T).astype(jnp.int32)
    t = w - T * cc
    x = slot & 3
    zh = (slot >> 2) & 3
    yh = (slot >> 4) & 1
    yl = slot >> 5
    z = zh * 2 + zpar
    return ((((yl * 2 + cc) * 4 + x) * 2 + yh) * 8 + z) * T + t


def group_rank(yh, z):
    k = (z >> 1) + (z & 1) * (4 + 2 * (1 - ((z >> 1) & 1)) - (z >> 1) + (z >> 2))
    return jnp.where((k & 1) == yh, k, 15 - k)


def rank_group(k):
    j = k if k < 8 else 15 - k
    z = 2 * j if j < 4 else (3, 7, 1, 5)[j - 4]
    yh = (j & 1) if k < 8 else 1 - (j & 1)
    return yh * 8 + z


def kernel(
    cut,
    len_ref, q_ref, k_ref, v_ref, qg_ref, kg_ref, out_ref,
    raw, halves, own_v, mates, perm, sb, ss, rel, rels, rb, rsh, rm, rmsh, ka, va, scr,
    obs, oshs, ob, osh, fin,
    ex_s, ex_r, main_s, main_r, fwd_s, fwd_r, sh_s, sh_r, fsh_s, fsh_r,
    rel_s, rel_r, rels_s, rels_r, o_s, o_r, osh_s, osh_r, fin_s, fin_r, fin_l, in_s,
):
    g = lax.axis_index("grp")
    x = lax.axis_index("uly")
    blk = lax.axis_index("blk")
    c = blk & 1
    yl = blk >> 1
    z = g & 7
    yh = g >> 3
    zp = z & 1
    zh = z >> 1
    slot = ((yl * 2 + yh) * 4 + zh) * 4 + x
    sgrp = slot >> 4
    xhalf = x >> 1
    xl_me = x & 1
    rank_me = group_rank(yh, z)
    short = rank_me >= cut
    three = yl == (zp ^ xl_me)
    mate = (g, x, yl * 2 + 1 - c)
    next_chip = (g, x, (1 - yl) * 2 + c)
    own = jnp.logical_and(xhalf == c, zp == c)

    def far_first(i):
        j = (i >> 2) & 7
        return (z + jnp.where((j & 1) == 0, 4 + (j >> 1), 3 - (j >> 1))) & 7

    def dest(i):
        xl = i & 1
        ty = yh ^ ((i >> 1) & 1)
        tz = far_first(i)
        y2 = yl ^ (i >> 5)
        return group_rank(ty, tz), xl, y2, ((ty << 3) | tz, 2 * c + xl, y2 * 2 + zp)

    def is_self(i):
        return jnp.logical_and(own, i == xl_me + 28)

    def source(s):
        return (
            (((s >> 4) & 1) << 3) | (((s >> 2) & 3) << 1) | c,
            s & 3,
            ((s >> 5) << 1) | xhalf,
        )

    def remote(src, dst, ssem, rsem, to):
        return pltpu.make_async_remote_copy(
            src_ref=src, dst_ref=dst, send_sem=ssem, recv_sem=rsem,
            device_id=to, device_id_type=MESH,
        )

    def send(src, dst, ssem, rsem, to, here):
        @pl.when(here)
        def _():
            pltpu.make_async_copy(src, dst, rsem).start()

        @pl.when(jnp.logical_not(here))
        def _():
            remote(src, dst, ssem, rsem, to).start()

    def wait_for(ref, sem):
        pltpu.make_async_copy(ref, ref, sem).wait()

    mine_cols = pl.ds(pl.multiple_of(c * HALF, HALF), HALF)
    mate_cols = pl.ds(pl.multiple_of((1 - c) * HALF, HALF), HALF)
    loads = [
        pltpu.make_async_copy(q_ref, raw.at[0], in_s.at[0]),
        pltpu.make_async_copy(k_ref, raw.at[1], in_s.at[1]),
        pltpu.make_async_copy(v_ref.at[:, :, mine_cols], own_v, in_s.at[2]),
    ]
    for load in loads:
        load.start()

    barrier = pltpu.get_barrier_semaphore()

    def greet(i, carry):
        @pl.when(jnp.logical_not(is_self(i)))
        def _():
            pl.semaphore_signal(barrier, inc=1, device_id=dest(i)[3], device_id_type=MESH)

        @pl.when(jnp.logical_not(jnp.logical_and(own, i == slot)))
        def _():
            pl.semaphore_signal(barrier, inc=1, device_id=source(i), device_id_type=MESH)

        return carry

    lax.fori_loop(0, SLOTS, greet, 0)
    pl.semaphore_signal(barrier, inc=1, device_id=mate, device_id_type=MESH)
    pl.semaphore_signal(barrier, inc=1, device_id=next_chip, device_id_type=MESH)

    sizes = [len_ref[i] for i in range(R)]
    ranks = []
    count = jnp.int32(0)
    for i in range(R):
        rank = jnp.int32(0)
        for j in range(R):
            if j != i:
                ahead = sizes[j] >= sizes[i] if j < i else sizes[j] > sizes[i]
                rank = rank + ahead.astype(jnp.int32)
        ranks.append(rank)
        count = count + jnp.where(rank == rank_me, sizes[i], 0)

    def norm_into(gain_ref, at):
        gain = gain_ref[...][None, :]
        for t in range(T):
            wide = raw[at, t].astype(F32)
            power = jnp.mean(wide * wide, axis=-1, keepdims=True)
            y = (wide * lax.rsqrt(power + 1e-06) * gain).astype(BF)
            halves[0, at, t] = y[:, :HALF]
            halves[1, at, t] = y[:, HALF:]

    loads[0].wait()
    norm_into(qg_ref, 0)

    @pl.when(own)
    def _():
        pl.semaphore_wait(barrier, 2 * SLOTS)

    @pl.when(jnp.logical_not(own))
    def _():
        pl.semaphore_wait(barrier, 2 * SLOTS + 2)

    exch = [
        remote(halves.at[1 - c, 0], mates.at[0], ex_s.at[0], ex_r.at[0], mate),
        remote(halves.at[1 - c, 1], mates.at[1], ex_s.at[1], ex_r.at[1], mate),
        remote(v_ref.at[:, :, mate_cols], mates.at[2], ex_s.at[2], ex_r.at[2], mate),
    ]
    exch[2].start()
    exch[0].start()
    loads[1].wait()
    norm_into(kg_ref, 1)
    exch[1].start()

    shape = (R, 2 * T, TILE)
    ow = lax.broadcasted_iota(jnp.int32, shape, 1)
    occ = (ow >= T).astype(jnp.int32)
    col = lax.broadcasted_iota(jnp.int32, (1, 1, TILE), 2)
    rank_of = jnp.zeros((1, 1, TILE), jnp.int32)
    for i in range(R):
        rank_of = jnp.where((col & 15) == i, ranks[i], rank_of)
    place_of = (col >> 4) + 64 * rank_of
    want = jnp.where(occ == c, 0, 1) * T + ow - T * occ
    want = want + 64 * lax.broadcasted_iota(jnp.int32, shape, 0)
    perm[...] = (want == place_of).astype(F32).reshape(TILE, TILE).astype(BF)

    loads[2].wait()
    for at in range(3):
        exch[at].wait()

    def pack(at, xl, first, width):
        cols = slice(xl * 640 + first * HD, xl * 640 + (first + width) * HD)
        mine = own_v[:, :, cols] if at == 2 else halves[c, at, :, :, cols]
        mine = mine.reshape(T * R, width * HD)
        theirs = mates[at, :, :, cols].reshape(T * R, width * HD)
        both = jnp.concatenate([mine, theirs], axis=0)
        res = jnp.dot(perm[...], both, preferred_element_type=F32)
        return res.reshape(R, 2 * T, width * HD)

    parts = ((0, 4, 0), (4, 12, 1), (12, 16, 0))

    for at in range(3):
        for xl in range(2):
            for hp in range(2):
                res = pack(at, xl, 3 * hp, 2)
                two = jnp.concatenate([res[:, :, :HD], res[:, :, HD:]], axis=1).astype(BF)
                for lo, hi, odd in parts:
                    sb[lo:hi, xl, hp ^ odd ^ xl, at * 48 : at * 48 + 48, :] = two[lo:hi]

    far_ranks = R - cut
    if far_ranks:
        @pl.when(yl == 0)
        def _():
            remote(sb.at[pl.ds(cut, far_ranks), :, 1], rel, rel_s, rel_r, next_chip).start()

    def send_main(i, carry):
        k, xl, y2, to = dest(i)
        ok = jnp.logical_or(k < cut, jnp.logical_and(yl == 0, y2 == 0))

        @pl.when(ok)
        def _():
            send(sb.at[k, xl, y2], rb.at[slot], main_s, main_r.at[sgrp], to, is_self(i))

        return carry

    lax.fori_loop(0, SLOTS, send_main, 0)

    for xl in range(2):
        kv = jnp.concatenate([pack(1, xl, 2, 1), pack(2, xl, 2, 1)], axis=1)
        ss[:, xl, 0:48, :] = kv.astype(BF)
        qq = jnp.concatenate([pack(0, xl, 2, 1), jnp.zeros((R, 8, HD), F32)], axis=1)
        ss[:, xl, 48:80, :] = qq.astype(BF)

    def pass_on(k, xl, src, dst, ssem, rsem):
        gk = rank_group(k)
        here = jnp.logical_and(own, jnp.logical_and(g == gk, xl_me == xl))
        send(src, dst, ssem, rsem, (gk, 2 * c + xl, 2 + zp), here)

    def spare(k):
        return 1 ^ (rank_group(k) & 1)

    if far_ranks:
        @pl.when(yl == 0)
        def _():
            for k in range(cut, R):
                at = k - cut
                remote(
                    ss.at[k, spare(k)], rels.at[at], rels_s.at[at], rels_r.at[at], next_chip
                ).start()

        @pl.when(yl == 1)
        def _():
            wait_for(rel, rel_r)
            for k in range(cut, R):
                for xl in range(2):
                    pass_on(
                        k, xl, rel.at[k - cut, xl], rb.at[slot & 31], main_s, main_r.at[yh]
                    )

    def send_shared(i, carry):
        xl = i & 1
        ty = yh ^ ((i >> 1) & 1)
        tz = far_first(i)
        k = group_rank(ty, tz)
        y2 = (tz & 1) ^ xl
        ok = jnp.logical_or(k < cut, jnp.logical_and(yl == 0, y2 == 0))
        here = jnp.logical_and(is_self(i), three)

        @pl.when(ok)
        def _():
            send(
                ss.at[k, xl], rsh.at[slot], sh_s, sh_r.at[sgrp],
                ((ty << 3) | tz, 2 * c + xl, y2 * 2 + zp), here,
            )

        return carry

    lax.fori_loop(0, SLOTS // 2, send_shared, 0)

    if far_ranks:
        @pl.when(yl == 1)
        def _():
            for k in range(cut, R):
                at = k - cut
                wait_for(rels.at[at], rels_r.at[at])
                pass_on(k, spare(k), rels.at[at], rsh.at[slot & 31], sh_s, sh_r.at[yh])

    lane0 = (lax.broadcasted_iota(jnp.int32, (SUB, HD), 1) == 0).astype(F32).astype(BF)

    def live_rows(slots, first, zpar):
        s = lax.broadcasted_iota(jnp.int32, (slots, 2 * T, HD), 0) + first
        flag = slot_pos((slots, 2 * T, HD), s, zpar) < count
        return flag.astype(F32).reshape(slots * 2 * T, HD)

    def masks(i, carry):
        flag = live_rows(16, (i & 3) * 16, jnp.where(i < 4, c, 1 - c))
        rows = pl.ds(pl.multiple_of(i * TILE, TILE), TILE)
        for h in range(3):
            ka[h, rows, HD:] = ((flag - 1.0) * 1e30).astype(BF)
            va[h, rows, HD:] = jnp.ones((TILE, HD), BF)
        return carry

    lax.fori_loop(0, 8, masks, 0)

    def place(ref, h, rows, value):
        ref[h, rows, :HD] = value.reshape(TILE, HD).astype(BF)

    def gather(some, arrived, forward, ours, theirs, heads):
        def lay(i, value):
            rows = slice(i * TILE, (i + 1) * TILE)
            kv = value.astype(F32)
            for n, h in enumerate(heads):
                place(ka, h, rows, kv[:, 24 * n : 24 * n + 24])
                m = n + len(heads)
                place(va, h, rows, kv[:, 24 * m : 24 * m + 24])

        def blank(i):
            rows = slice(i * TILE, (i + 1) * TILE)
            for h in heads:
                ka[h, rows, :HD] = jnp.zeros((TILE, HD), BF)
                va[h, rows, :HD] = jnp.zeros((TILE, HD), BF)

        def first(i):
            arrived(i)
            forward(i).start()
            lay(i, ours(i))

        def second(i):
            forward(i).wait()
            lay(4 + i, theirs(i))

        for step, shift in ((first, 0), (second, 4)):
            for i in range(4):
                if i < 2 or not some:
                    step(i)
                else:
                    @pl.when(short)
                    def _(i=i, shift=shift):
                        blank(shift + i)

                    @pl.when(jnp.logical_not(short))
                    def _(i=i, step=step):
                        step(i)

    def grp(i):
        return pl.ds(16 * i, 16)

    gather(
        far_ranks,
        lambda i: wait_for(rb.at[grp(i)], main_r.at[i]),
        lambda i: remote(
            rb.at[grp(i), pl.ds(48, 96)], rm.at[grp(i)], fwd_s.at[i], fwd_r.at[i], mate
        ),
        lambda i: rb[16 * i : 16 * i + 16, 48:144, :],
        lambda i: rm[16 * i : 16 * i + 16],
        (0, 1),
    )

    scale = HD ** (-0.5) * LOG2E

    def attend(q, h, live):
        step = 512
        outs = []
        for n in range(BLOCK // SUB):
            rows = slice(n * SUB, (n + 1) * SUB)
            qa = jnp.concatenate([q[rows], lane0], axis=1)
            top = None
            for j in range(KEYS // step):
                cols = slice(j * step, (j + 1) * step)
                part = lax.dot_general(
                    qa, ka[h, cols, :], (((1,), (1,)), ((), ())),
                    preferred_element_type=F32,
                )
                scr[rows, cols] = part
                for i in range(step // HD):
                    piece = part[:, i * HD : (i + 1) * HD]
                    top = piece if top is None else jnp.maximum(top, piece)
            peak = jnp.max(top, axis=1, keepdims=True)
            mixed = None
            for j in range(KEYS // step):
                cols = slice(j * step, (j + 1) * step)
                weights = jnp.exp2((scr[rows, cols] - peak) * scale).astype(BF)
                part = jnp.dot(weights, va[h, cols, :], preferred_element_type=F32)
                mixed = part if mixed is None else mixed + part
            outs.append(jnp.where(live[rows] > 0.0, mixed[:, :HD] / mixed[:, HD:], 0.0))
        return jnp.concatenate(outs, axis=0)

    passes = jnp.where(short, 1, 2)

    def back_from(ref, to, ssem, rsem, first):
        def back(j, carry):
            s = first + (j ^ (slot & 31))
            here = jnp.logical_and(own, s == slot)
            send(ref.at[s], to, ssem, rsem, source(s), here)
            return carry

        lax.fori_loop(0, 32, back, 0)

    def main_pass(i, carry):
        at = pl.ds(pl.multiple_of(i * 32, 32), 32)
        live = live_rows(32, i * 32, c)
        qq = rb[at, 0:48, :].astype(F32)
        res = []
        for h in range(2):
            q = qq[:, 24 * h : 24 * h + 24].reshape(BLOCK, HD).astype(BF)
            res.append(attend(q, h, live).reshape(32, 2 * T, HD))
        obs[at] = jnp.concatenate(res, axis=1).astype(BF)
        rsem = o_r.at[xl_me, short.astype(jnp.int32)]
        back_from(obs, ob.at[rank_me, xl_me, yl], o_s, rsem, i * 32)
        return carry

    lax.fori_loop(0, passes, main_pass, 0)

    def third_pass(i, carry):
        at = pl.ds(pl.multiple_of(i * 32, 32), 32)
        live = live_rows(32, i * 32, c)
        q = rsh[at, 48:80, :].astype(F32)[:, 0:24].reshape(BLOCK, HD).astype(BF)
        res = attend(q, 2, live).reshape(32, 2 * T, HD)
        oshs[at] = jnp.concatenate([res, jnp.zeros((32, 8, HD), F32)], axis=1).astype(BF)
        rsem = osh_r.at[xl_me, short.astype(jnp.int32)]
        back_from(oshs, osh.at[rank_me, xl_me], osh_s, rsem, i * 32)
        return carry

    def sent_back(ref, sem):
        whole = jnp.logical_not(short)
        one = jnp.logical_and(own, jnp.logical_or(whole, yl == 0))
        for n, kind in ((SLOTS, whole), (SLOTS // 2, short)):
            if n == SLOTS or far_ranks:
                @pl.when(jnp.logical_and(kind, one))
                def _(n=n):
                    wait_for(ref.at[pl.ds(0, n - 1)], sem)

                @pl.when(jnp.logical_and(kind, jnp.logical_not(one)))
                def _(n=n):
                    wait_for(ref.at[pl.ds(0, n)], sem)

    @pl.when(three)
    def _():
        gather(
            far_ranks,
            lambda i: wait_for(rsh.at[grp(i)], sh_r.at[i]),
            lambda i: remote(
                rsh.at[grp(i), pl.ds(0, 48)], rmsh.at[grp(i)], fsh_s.at[i], fsh_r.at[i], mate
            ),
            lambda i: rsh[16 * i : 16 * i + 16, 0:48, :],
            lambda i: rmsh[16 * i : 16 * i + 16],
            (2,),
        )
        lax.fori_loop(0, passes, third_pass, 0)
        sent_back(oshs, osh_s)

    sent_back(obs, o_s)
    n_main = SLOTS - 2 * far_ranks
    n_shared = SLOTS // 2 - far_ranks

    def sent(ref, n, sem, one):
        @pl.when(one)
        def _():
            wait_for(ref.at[pl.ds(0, n - 1)], sem)

        @pl.when(jnp.logical_not(one))
        def _():
            wait_for(ref.at[pl.ds(0, n)], sem)

    sent(rb, n_main, main_s, own)
    sent(rsh, n_shared, sh_s, jnp.logical_and(own, three))
    if far_ranks:
        @pl.when(yl == 0)
        def _():
            wait_for(rel, rel_s)
            for at in range(far_ranks):
                wait_for(rels.at[at], rels_s.at[at])

    def unpack(value):
        res = lax.dot_general(
            perm[...], value, (((0,), (0,)), ((), ())), preferred_element_type=F32
        )
        return res.astype(BF)

    def store(res, xl, first, width):
        cols = slice(xl * 640 + first * HD, xl * 640 + (first + width) * HD)
        fin[0, :, :, cols] = res[: T * R].reshape(T, R, width * HD)
        fin[1, :, :, cols] = res[T * R :].reshape(T, R, width * HD)

    def returned(ref, sem, xl):
        wait_for(ref.at[pl.ds(0, cut), xl], sem.at[xl, 0])
        if far_ranks:
            @pl.when(yl == 0)
            def _():
                wait_for(ref.at[pl.ds(cut, far_ranks), xl], sem.at[xl, 1])

            @pl.when(yl == 1)
            def _():
                ref[cut:, xl] = jnp.zeros(ref[cut:, xl].shape, BF)

    done = []

    def ship(first, width):
        n = len(done)
        at = pl.ds(pl.multiple_of(c * HALF + first, HD), width)
        here = pl.ds(first, width)
        far = remote(
            fin.at[1, :, :, here], out_ref.at[:, :, at], fin_s.at[n], fin_r.at[n], mate
        )
        far.start()
        near = pltpu.make_async_copy(fin.at[0, :, :, here], out_ref.at[:, :, at], fin_l.at[n])
        near.start()
        done.append((far, near))

    for xl in range(2):
        returned(ob, o_r, xl)
        for hp in range(2):
            got = jnp.concatenate(
                [ob[lo:hi, xl, hp ^ odd ^ xl] for lo, hi, odd in parts], axis=0
            ).astype(F32)
            flat = [got[:, 24 * h : 24 * h + 24].reshape(TILE, HD) for h in range(2)]
            store(unpack(jnp.concatenate(flat, axis=1).astype(BF)), xl, 3 * hp, 2)
            ship(xl * 640 + 384 * hp, 256)
    for xl in range(2):
        returned(osh, osh_r, xl)
        got = osh[:, xl].astype(F32)[:, 0:24].reshape(TILE, HD)
        store(unpack(got.astype(BF)), xl, 2, 1)
        ship(xl * 640 + 256, 128)
    for far, near in done:
        far.wait()
        near.wait()


def run(cut, lengths, q, k, v, q_gain, k_gain):
    vm = pl.BlockSpec(memory_space=pltpu.VMEM)
    hbm = pl.BlockSpec(memory_space=pl.ANY)
    dma = pltpu.SemaphoreType.DMA
    far = max(R - cut, 1)
    scratch = [
        pltpu.VMEM((2, T, R, 2 * HALF), BF),
        pltpu.VMEM((2, 2, T, R, HALF), BF),
        pltpu.VMEM((T, R, HALF), BF),
        pltpu.VMEM((3, T, R, HALF), BF),
        pltpu.VMEM((TILE, TILE), BF),
        pltpu.VMEM((R, 2, 2, 144, HD), BF),
        pltpu.VMEM((R, 2, 80, HD), BF),
        pltpu.VMEM((far, 2, 144, HD), BF),
        pltpu.VMEM((far, 80, HD), BF),
        pltpu.VMEM((SLOTS, 144, HD), BF),
        pltpu.VMEM((SLOTS, 80, HD), BF),
        pltpu.VMEM((SLOTS, 96, HD), BF),
        pltpu.VMEM((SLOTS, 48, HD), BF),
        pltpu.VMEM((3, KEYS, 2 * HD), BF),
        pltpu.VMEM((3, KEYS, 2 * HD), BF),
        pltpu.VMEM((BLOCK, KEYS), F32),
        pltpu.VMEM((SLOTS, 48, HD), BF),
        pltpu.VMEM((SLOTS, 32, HD), BF),
        pltpu.VMEM((R, 2, 2, 48, HD), BF),
        pltpu.VMEM((R, 2, 32, HD), BF),
        pltpu.VMEM((2, T, R, HALF), BF),
        dma((3,)), dma((3,)),
        dma, dma((4,)),
        dma((4,)), dma((4,)),
        dma, dma((4,)),
        dma((4,)), dma((4,)),
        dma, dma, dma((far,)), dma((far,)),
        dma, dma((2, 2)),
        dma, dma((2, 2)),
        dma((6,)), dma((6,)), dma((6,)),
        dma((3,)),
    ]
    return pl.pallas_call(
        functools.partial(kernel, cut),
        out_shape=jax.ShapeDtypeStruct((T, R, 2 * HALF), BF),
        in_specs=[pl.BlockSpec(memory_space=pltpu.SMEM), hbm, hbm, hbm, vm, vm],
        out_specs=pl.BlockSpec(memory_space=pl.ANY),
        scratch_shapes=scratch,
        compiler_params=pltpu.CompilerParams(
            collective_id=cut, has_side_effects=True, vmem_limit_bytes=60 << 20
        ),
        name="attend_%d" % cut,
    )(lengths, q, k, v, q_gain, k_gain)


def per_device(q_in, k_in, v_in, q_gain, k_gain, lengths):
    args = (
        lengths,
        jnp.transpose(q_in, (1, 0, 2)),
        jnp.transpose(k_in, (1, 0, 2)),
        jnp.transpose(v_in, (1, 0, 2)),
        q_gain,
        k_gain,
    )
    fits = jnp.sum((lengths > REACH).astype(jnp.int32)) <= CUT
    res = lax.cond(
        fits,
        functools.partial(run, CUT),
        functools.partial(run, R),
        *args,
    )
    return jnp.transpose(res, (1, 0, 2))


def solution(mesh):
    placed = P(None, ("grp", "uly", "blk"), None)
    return jax.shard_map(
        per_device,
        mesh=mesh,
        in_specs=(placed, placed, placed, P(), P(), P()),
        out_specs=placed,
        check_vma=False,
    )
```

profile of v0, /device:TPU:31, one launch (start us, length us, event | category | flops | bytes accessed | tf_op | source)
XLA Modules:
  0.0 111.5 jit_solution(14760442129778297419)
XLA Ops:
  0.0 1.3 %fusion = s32[]{:T(128)} fusion(s32[16]{0:T(128)} %param.13), kind=kLoop, calls=%fused_computation.1 | loop fusion | flops 47 | bytes 68 | tf_op jit(solution)/shard_map/reduce_sum | solution.py:603
  1.9 0.0 copy-start
  2.0 0.6 copy-done
  2.6 108.0 %conditional.1 = (bf16[12,16,2560]{2,1,0:T(8,128)(2,1)S(1)}) conditional(s32[]{:T(128)} %convert_element_type.7, (s32[16]{0:T(128)S(1)}, bf16[12,16,2560]{2,1,0:T(8,128)(2,1)}, bf16[12,16,2560]{2,1,0:T(8,128)(2,1)}, bf16[12,16,2560]{2,1,0:T(8,128)(2,1)}, f32[2560]{0:T(1024)}, /*index=5*/f32[2560]{0:T(1024)}) %tuple.20, (s32[16]{0:T(128)S(1)}, ...), branch_computations={%region_1.0_spmd, %region_2.0_spmd} | conditional | bytes 8 | solution.py:604
  2.6 107.6 %attend_10.1 = bf16[12,16,2560]{2,1,0:T(8,128)(2,1)S(1)} custom-call(s32[16]{0:T(128)S(1)} %get-tuple-element.38.len_ref, bf16[12,16,2560]{2,1,0:T(8,128)(2,1)} %get-tuple-element.39.q_ref, bf16[12,16,2560]{2,1,0:T(8,128)(2,1)} %get-tuple-element.40.k_ref, bf16[12,16,2560]{2,1,0:T(8,128)(2,1)} %get-tuple-element.41.v_ref, f32[2560]{0:T(1024)} %get-tuple-element.42.qg_ref, ...), custom_call_target="tpu_custom_call" | custom-call | tf_op jit(solution)/shard_map/cond/branch_1_fun/attend_10/pallas_call | solution.py:581
  110.6 0.9 copy.10
Async XLA Ops:
  1.9 0.7 copy-start
where the time goes:
time: 112 us
  Pallas kernels  108 us (96%)
  local copies, waits for them, and re-layouts  1.6 us (1%)
  other arithmetic  1.29 us (1%)
    pallas_call x1, Pallas kernels, run(): pl.pallas_call(functools.partial(kernel, cut), out_shape=jax.ShapeDtypeSt...  108 us

commit v1 on v0

--- a/solution.py
+++ b/solution.py
@@ -51,8 +51,8 @@
 
 def kernel(
     cut,
-    len_ref, q_ref, k_ref, v_ref, qg_ref, kg_ref, out_ref,
-    raw, halves, own_v, mates, perm, sb, ss, rel, rels, rb, rsh, rm, rmsh, ka, va, scr,
+    len_hbm, q_ref, k_ref, v_ref, qg_ref, kg_ref, out_ref,
+    len_ref, raw, halves, own_v, mates, perm, sb, ss, rel, rels, rb, rsh, rm, rmsh, ka, va, scr,
     obs, oshs, ob, osh, fin,
     ex_s, ex_r, main_s, main_r, fwd_s, fwd_r, sh_s, sh_r, fsh_s, fsh_r,
     rel_s, rel_r, rels_s, rels_r, o_s, o_r, osh_s, osh_r, fin_s, fin_r, fin_l, in_s,
@@ -78,18 +78,18 @@
     own = jnp.logical_and(xhalf == c, zp == c)
 
     def far_first(i):
-        j = (i >> 2) & 7
+        j = i & 7
         return (z + jnp.where((j & 1) == 0, 4 + (j >> 1), 3 - (j >> 1))) & 7
 
     def dest(i):
-        xl = i & 1
-        ty = yh ^ ((i >> 1) & 1)
-        tz = far_first(i)
-        y2 = yl ^ (i >> 5)
+        y2 = yl ^ (i & 1)
+        xl = (i >> 1) & 1
+        ty = yh ^ ((i >> 2) & 1)
+        tz = far_first(i >> 3)
         return group_rank(ty, tz), xl, y2, ((ty << 3) | tz, 2 * c + xl, y2 * 2 + zp)
 
     def is_self(i):
-        return jnp.logical_and(own, i == xl_me + 28)
+        return jnp.logical_and(own, i == 2 * xl_me + 56)
 
     def source(s):
         return (
@@ -122,6 +122,7 @@
         pltpu.make_async_copy(q_ref, raw.at[0], in_s.at[0]),
         pltpu.make_async_copy(k_ref, raw.at[1], in_s.at[1]),
         pltpu.make_async_copy(v_ref.at[:, :, mine_cols], own_v, in_s.at[2]),
+        pltpu.make_async_copy(len_hbm, len_ref, in_s.at[3]),
     ]
     for load in loads:
         load.start()
@@ -143,6 +144,7 @@
     pl.semaphore_signal(barrier, inc=1, device_id=mate, device_id_type=MESH)
     pl.semaphore_signal(barrier, inc=1, device_id=next_chip, device_id_type=MESH)
 
+    loads[3].wait()
     sizes = [len_ref[i] for i in range(R)]
     ranks = []
     count = jnp.int32(0)
@@ -274,11 +276,11 @@
     def send_shared(i, carry):
         xl = i & 1
         ty = yh ^ ((i >> 1) & 1)
-        tz = far_first(i)
+        tz = far_first(i >> 2)
         k = group_rank(ty, tz)
         y2 = (tz & 1) ^ xl
         ok = jnp.logical_or(k < cut, jnp.logical_and(yl == 0, y2 == 0))
-        here = jnp.logical_and(is_self(i), three)
+        here = jnp.logical_and(jnp.logical_and(own, three), i == xl_me + 28)
 
         @pl.when(ok)
         def _():
@@ -461,29 +463,6 @@
             (2,),
         )
         lax.fori_loop(0, passes, third_pass, 0)
-        sent_back(oshs, osh_s)
-
-    sent_back(obs, o_s)
-    n_main = SLOTS - 2 * far_ranks
-    n_shared = SLOTS // 2 - far_ranks
-
-    def sent(ref, n, sem, one):
-        @pl.when(one)
-        def _():
-            wait_for(ref.at[pl.ds(0, n - 1)], sem)
-
-        @pl.when(jnp.logical_not(one))
-        def _():
-            wait_for(ref.at[pl.ds(0, n)], sem)
-
-    sent(rb, n_main, main_s, own)
-    sent(rsh, n_shared, sh_s, jnp.logical_and(own, three))
-    if far_ranks:
-        @pl.when(yl == 0)
-        def _():
-            wait_for(rel, rel_s)
-            for at in range(far_ranks):
-                wait_for(rels.at[at], rels_s.at[at])
 
     def unpack(value):
         res = lax.dot_general(
@@ -539,6 +518,33 @@
         far.wait()
         near.wait()
 
+    sent_back(obs, o_s)
+
+    @pl.when(three)
+    def _():
+        sent_back(oshs, osh_s)
+
+    n_main = SLOTS - 2 * far_ranks
+    n_shared = SLOTS // 2 - far_ranks
+
+    def sent(ref, n, sem, one):
+        @pl.when(one)
+        def _():
+            wait_for(ref.at[pl.ds(0, n - 1)], sem)
+
+        @pl.when(jnp.logical_not(one))
+        def _():
+            wait_for(ref.at[pl.ds(0, n)], sem)
+
+    sent(rb, n_main, main_s, own)
+    sent(rsh, n_shared, sh_s, jnp.logical_and(own, three))
+    if far_ranks:
+        @pl.when(yl == 0)
+        def _():
+            wait_for(rel, rel_s)
+            for at in range(far_ranks):
+                wait_for(rels.at[at], rels_s.at[at])
+
 
 def run(cut, lengths, q, k, v, q_gain, k_gain):
     vm = pl.BlockSpec(memory_space=pltpu.VMEM)
@@ -546,6 +552,7 @@
     dma = pltpu.SemaphoreType.DMA
     far = max(R - cut, 1)
     scratch = [
+        pltpu.SMEM((R,), jnp.int32),
         pltpu.VMEM((2, T, R, 2 * HALF), BF),
         pltpu.VMEM((2, 2, T, R, HALF), BF),
         pltpu.VMEM((T, R, HALF), BF),
@@ -576,12 +583,12 @@
         dma, dma((2, 2)),
         dma, dma((2, 2)),
         dma((6,)), dma((6,)), dma((6,)),
-        dma((3,)),
+        dma((4,)),
     ]
     return pl.pallas_call(
         functools.partial(kernel, cut),
         out_shape=jax.ShapeDtypeStruct((T, R, 2 * HALF), BF),
-        in_specs=[pl.BlockSpec(memory_space=pltpu.SMEM), hbm, hbm, hbm, vm, vm],
+        in_specs=[hbm, hbm, hbm, hbm, vm, vm],
         out_specs=pl.BlockSpec(memory_space=pl.ANY),
         scratch_shapes=scratch,
         compiler_params=pltpu.CompilerParams(

time: 112 us -> 111 us (level)
  Pallas kernels: 108 us -> 106 us
    pallas_call x1, Pallas kernels: 108 us -> 106 us  [run(): pl.pallas_call(functools.partial(kernel, cut), out_shape=jax.ShapeDtypeSt...]
where the time goes in v1:
time: 111 us; the launch traced here: 110 us
  Pallas kernels  106 us (95%)
  local copies, waits for them, and re-layouts  1.6 us (1%)
  other arithmetic  1.29 us (1%)
    pallas_call x1, Pallas kernels, run(): pl.pallas_call(functools.partial(kernel, cut), out_shape=jax.ShapeDtypeSt...  106 us

profile of v1, /device:TPU:31, one launch (start us, length us, event | category | flops | bytes accessed | tf_op | source)
XLA Modules:
  0.0 110.2 jit_solution(5139986094278984634)
XLA Ops:
  0.0 1.3 %fusion = s32[]{:T(128)} fusion(s32[16]{0:T(128)} %param.13), kind=kLoop, calls=%fused_computation.1 | loop fusion | flops 47 | bytes 68 | tf_op jit(solution)/shard_map/reduce_sum | solution.py:610
  1.9 0.0 copy-start
  2.0 0.6 copy-done
  2.6 106.7 %conditional.1 = (bf16[12,16,2560]{2,1,0:T(8,128)(2,1)S(1)}) conditional(s32[]{:T(128)} %convert_element_type.7, (s32[16]{0:T(128)S(1)}, bf16[12,16,2560]{2,1,0:T(8,128)(2,1)}, bf16[12,16,2560]{2,1,0:T(8,128)(2,1)}, bf16[12,16,2560]{2,1,0:T(8,128)(2,1)}, f32[2560]{0:T(1024)}, /*index=5*/f32[2560]{0:T(1024)}) %tuple.20, (s32[16]{0:T(128)S(1)}, ...), branch_computations={%region_1.0_spmd, %region_2.0_spmd} | conditional | bytes 8 | solution.py:611
  2.6 106.3 %attend_10.1 = bf16[12,16,2560]{2,1,0:T(8,128)(2,1)S(1)} custom-call(s32[16]{0:T(128)S(1)} %get-tuple-element.38.len_hbm, bf16[12,16,2560]{2,1,0:T(8,128)(2,1)} %get-tuple-element.39.q_ref, bf16[12,16,2560]{2,1,0:T(8,128)(2,1)} %get-tuple-element.40.k_ref, bf16[12,16,2560]{2,1,0:T(8,128)(2,1)} %get-tuple-element.41.v_ref, f32[2560]{0:T(1024)} %get-tuple-element.42.qg_ref, ...), custom_call_target="tpu_custom_call" | custom-call | tf_op jit(solution)/shard_map/cond/branch_1_fun/attend_10/pallas_call | solution.py:588
  109.3 0.9 copy.10
Async XLA Ops:
  1.9 0.7 copy-start
